TPU v7x, 256 devices: a whole 4x4x8 slice. The times are simulated.
256 devices in a mesh: ind: 8 (over x, core), var: 32 (over z, y).
Axes of the slice: x: 4, y: 4, z: 8, core: 2. Of those that a mesh axis runs over, the one named last changes fastest.
Arguments:
- dosages: bfloat16 [131072, 8192], P('ind', 'var'), may hold values from -4 to 4
- phenotypes: float32 [32, 131072], P(None, 'ind'), may hold values from -6 to 6
- screen_ids: int32 [32, 256], P('var'), may hold values from 0 to 255, each once within a row
- screen_counts: int32 [32], P('var'), may hold values from 1 to 192, 2048 in all
- kkt_ids: int32 [32, 64], P('var'), may hold values from 0 to 255
- coef_prev: float32 [32, 6144], P(None, 'var'), may hold values from -3 to 3
- coef_slope: float32 [32, 6144], P(None, 'var'), may hold values from -3 to 3
- penalty: float32 [32], replicated, may hold values from 0.02 to 0.4
Outputs:
- coefficients: float32 [32, 6144], P(None, 'var')
- residual: float32 [32, 131072], P(None, ('ind', 'var'))
- kkt_grad: float32 [32, 2048], P(None, 'var')
- max_violation: float32 [32], replicated
- objective: float32 [32], replicated
Inputs may be any that keep to these rules, and one draw needn't show every extreme that they name: `screen_ids`: each row names every one of the owner's 256 candidate columns once. `screen_counts`: the counts sum to 2048; some owner has exactly 192 live slots.
All inputs are finite; a program needn't handle non-finite values. No bound on the sum of `screen_counts` on one device may be relied on, other than what follows from the above.
Results may differ from a plain program's by a relative error of at most 0.0051.
Values may be sent and summed in bfloat16 or wider, within the bound.
A program may use at most 128 MiB of HBM per device.

v0:
```python
import jax
import jax.numpy as jnp
from jax import lax
from jax.sharding import PartitionSpec as P

SWEEPS = 2


def proximal(coef, grad, live, shrink, ridge):
    moved = coef + 0.5 * grad
    return live * jnp.sign(moved) * jnp.maximum(jnp.abs(moved) - shrink, 0.0) / ridge


def body(dosages, phenotypes, screen_ids, screen_counts, kkt_ids, coef_prev, coef_slope, penalty):
    cap = coef_prev.shape[1]
    row_dev = dosages.shape[0]
    total_rows = row_dev * lax.axis_size("ind")
    share = row_dev // lax.axis_size("var")
    start = lax.axis_index("var") * share
    screened = jnp.take(dosages, screen_ids[0, :cap], axis=1)
    kkt_cols = jnp.take(dosages, kkt_ids[0], axis=1)
    live = (jnp.arange(cap, dtype=jnp.int32) < screen_counts[0]).astype(jnp.float32)[None, :]
    shrink = 0.25 * penalty[:, None]
    ridge = 1.0 + 0.25 * penalty[:, None]
    coef = live * (coef_prev + 0.5 * coef_slope)

    def residual_of(current):
        partial_value = lax.dot_general(
            current.astype(jnp.bfloat16),
            screened,
            (((1,), (1,)), ((), ())),
            preferred_element_type=jnp.float32,
        )
        pred = lax.psum(partial_value, "var")
        resid = phenotypes - pred
        resid_bf = resid.astype(jnp.bfloat16)
        resid_share = lax.dynamic_slice_in_dim(resid, start, share, 1)
        return (resid_share, resid_bf)

    for sweep in range(SWEEPS):
        resid_share, resid_bf = residual_of(coef)
        partial_grad = lax.dot_general(
            resid_bf, screened, (((1,), (0,)), ((), ())), preferred_element_type=jnp.float32
        )
        grad = lax.psum(partial_grad, "ind") / total_rows
        coef = proximal(coef, grad, live, shrink, ridge)
    resid_share, resid_bf = residual_of(coef)
    kkt_partial = lax.dot_general(
        resid_bf, kkt_cols, (((1,), (0,)), ((), ())), preferred_element_type=jnp.float32
    )
    kkt_grad = lax.psum(kkt_partial, "ind") / total_rows
    local_worst = jnp.max(jnp.maximum(jnp.abs(kkt_grad) - 0.5 * penalty[:, None], 0.0), axis=1)
    max_violation = lax.pmax(local_worst, "var")
    loss_part = jnp.sum(resid_share * resid_share, axis=1) / (2.0 * total_rows)
    first_row = (lax.axis_index("ind") == 0).astype(jnp.float32)
    pen_part = first_row * penalty * jnp.sum(0.5 * jnp.abs(coef) + 0.25 * coef * coef, axis=1)
    loss_total, pen_total = lax.psum((loss_part, pen_part), ("ind", "var"))
    return (coef, resid_share, kkt_grad, max_violation, loss_total + pen_total)


def solution(mesh):
    placed = (
        P("ind", "var"),
        P(None, "ind"),
        P("var", None),
        P("var"),
        P("var", None),
        P(None, "var"),
        P(None, "var"),
        P(),
    )
    return jax.shard_map(
        body,
        mesh=mesh,
        in_specs=placed,
        out_specs=(P(None, "var"), P(None, ("ind", "var")), P(None, "var"), P(), P()),
        check_vma=False,
    )
```

profile of v0, /device:TPU:8, one launch (start us, length us, event | category | flops | bytes accessed | tf_op | source)
XLA Modules:
  0.0 751.4 jit_solution(5003248519054964283)
XLA Ops:
  7.2 0.0 all-reduce.4.cloned.1.call-start
  7.9 0.7 compare_select_fusion
  8.5 0.0 copy-start.5
  8.6 11.9 %copy.15 = bf16[16384,256]{0,1:T(8,128)(2,1)} copy(bf16[16384,256]{1,0:T(8,128)(2,1)} %param.8) | data formatting | bytes 16777216 | tf_op args[0]
  20.4 0.0 copy-done.5
  20.4 0.0 copy-start.3
  20.5 0.0 copy-start.4
  20.5 17.2 %gather_fusion = bf16[192,16384]{1,0:T(8,128)(2,1)} fusion(bf16[16384,256]{0,1:T(8,128)(2,1)} %copy.15, s32[1024]{0:T(1024)S(1)} %pad_clamp_fusion.1), kind=kCustom, calls=%fused_computation | custom fusion | bytes 12583680 | tf_op jit(solution)/shard_map/jit(_take)/gather | solution.py:20
  37.6 0.0 copy-done.3
  37.6 0.0 copy-done.4
  37.6 0.0 copy-start.6
  37.6 0.0 copy-start.1
  37.6 5.9 fusion.13
  43.5 0.0 all-reduce.4.cloned.1.call-update
  43.5 0.0 all-reduce.6.cloned.1.call-start
  43.6 0.0 copy-done.6
  43.6 155.8 %all-reduce.4.cloned.1.call-done = f32[32,16384]{1,0:T(8,128)} async-done(((f32[32,16384]{1,0:T(8,128)}), f32[32,16384]{1,0:T(8,128)}) %all-reduce.4.cloned.1.call-update) | async-done | bytes 2097168 | tf_op jit(solution)/shard_map/psum | solution.py:34
  199.4 0.0 copy-done.1
  199.4 5.6 fusion.3
  204.9 23.6 %psum.57 = f32[32,192]{1,0:T(8,128)S(1)} all-reduce(f32[32,192]{1,0:T(8,128)S(1)} %fusion.3), channel_id=1, replica_groups=mesh['ind'=8,'var'=32] {'ind'}, use_global_device_ids=true, to_apply=%region_1.2 | all-reduce | flops 6144 | bytes 49152 | tf_op jit(solution)/shard_map/psum | solution.py:45
  228.6 0.1 multiply_divide_fusion.1
  228.6 5.6 fusion.11
  234.2 0.0 all-reduce.6.cloned.1.call-update
  234.2 0.0 all-reduce.8.cloned.1.call-start
  234.3 148.9 %all-reduce.6.cloned.1.call-done = f32[32,16384]{1,0:T(8,128)} async-done(((f32[32,16384]{1,0:T(8,128)}), f32[32,16384]{1,0:T(8,128)}) %all-reduce.6.cloned.1.call-update) | async-done | bytes 2097168 | tf_op jit(solution)/shard_map/psum | solution.py:34
  383.2 5.5 fusion.4
  388.7 23.6 %psum.59 = f32[32,192]{1,0:T(8,128)S(1)} all-reduce(f32[32,192]{1,0:T(8,128)S(1)} %fusion.4), channel_id=1, replica_groups=mesh['ind'=8,'var'=32] {'ind'}, use_global_device_ids=true, to_apply=%region_3.4 | all-reduce | flops 6144 | bytes 49152 | tf_op jit(solution)/shard_map/psum | solution.py:45
  412.3 0.2 fusion.8
  412.5 0.0 copy-start.2
  412.5 0.0 copy-start.7
  412.5 5.6 fusion.9
  418.1 0.0 copy-done.2
  418.1 0.0 all-reduce.8.cloned.1.call-update
  418.1 0.0 copy-done.7
  418.2 8.1 %gather_fusion.1 = bf16[64,16384]{1,0:T(8,128)(2,1)S(1)} fusion(bf16[16384,256]{0,1:T(8,128)(2,1)} %copy.15, s32[1024]{0:T(1024)S(1)} %pad_clamp_fusion), kind=kCustom, calls=%fused_computation.1 | custom fusion | bytes 4194560 | tf_op jit(solution)/shard_map/jit(_take)/gather | solution.py:21
  426.3 140.6 %all-reduce.8.cloned.1.call-done = f32[32,16384]{1,0:T(8,128)} async-done(((f32[32,16384]{1,0:T(8,128)}), f32[32,16384]{1,0:T(8,128)}) %all-reduce.8.cloned.1.call-update) | async-done | bytes 2097168 | tf_op jit(solution)/shard_map/psum | solution.py:34
  566.9 2.4 sub.36
  569.4 0.0 copy-start
  569.4 1.3 copy-done
  570.7 0.7 multiply_reduce_fusion
  571.5 74.1 %psum.64 = f32[32]{0:T(128)} all-reduce(f32[32]{0:T(128)S(1)} %get-tuple-element.11), channel_id=1, replica_groups=mesh['ind'=8,'var'=32] {'ind','var'}, use_global_device_ids=true, to_apply=%region_9.10 | all-reduce | flops 32 | bytes 256 | tf_op jit(solution)/shard_map/psum | solution.py:57
  645.6 2.3 fusion
  647.9 24.8 %psum.61 = f32[32,64]{1,0:T(8,128)S(1)} all-reduce(f32[32,64]{1,0:T(8,128)S(1)} %fusion), channel_id=1, replica_groups=mesh['ind'=8,'var'=32] {'ind'}, use_global_device_ids=true, to_apply=%region_5.6 | all-reduce | flops 2048 | bytes 16384 | tf_op jit(solution)/shard_map/psum | solution.py:51
  672.7 0.7 maximum_reduce_fusion
  673.4 71.5 %pmax.7 = f32[32]{0:T(128)} all-reduce(f32[32]{0:T(128)S(1)} %get-tuple-element.9), channel_id=1, replica_groups=mesh['ind'=8,'var'=32] {'var'}, use_global_device_ids=true, to_apply=%region_7.8 | all-reduce | flops 32 | bytes 256 | tf_op jit(solution)/shard_map/pmax | solution.py:53
  (7 shorter events, 0.0 us)
Async XLA Ops:
  7.2 192.2 %all-reduce.4.cloned.1.call-start = ((), (), s32[]{:S(2)}) async-start(), calls=%async_computation | async-start | bytes 4194304 | tf_op jit(solution)/shard_map/psum | solution.py:34
  8.5 11.9 %copy-start.5 = (s32[1,256]{1,0:T(1,128)S(1)}, s32[1,256]{1,0:T(1,128)}, u32[]{:S(2)}) copy-start(s32[1,256]{1,0:T(1,128)} %param.10) | copy-start | bytes 3076
  20.4 17.2 %copy-start.3 = (f32[32,192]{1,0:T(8,128)S(1)}, f32[32,192]{1,0:T(8,128)}, u32[]{:S(2)}) copy-start(f32[32,192]{1,0:T(8,128)} %param.13) | copy-start | bytes 73732
  20.5 17.2 %copy-start.4 = (f32[32,192]{1,0:T(8,128)S(1)}, f32[32,192]{1,0:T(8,128)}, u32[]{:S(2)}) copy-start(f32[32,192]{1,0:T(8,128)} %param.14) | copy-start | bytes 73732
  37.6 5.9 copy-start.6
  37.6 161.8 %copy-start.1 = (f32[32,16384]{1,0:T(8,128)S(1)}, f32[32,16384]{1,0:T(8,128)}, u32[]{:S(2)}) copy-start(f32[32,16384]{1,0:T(8,128)} %param.9) | copy-start | bytes 6291460
  43.5 339.6 %all-reduce.6.cloned.1.call-start = ((), (), s32[]{:S(2)}) async-start(), calls=%async_computation.1 | async-start | bytes 4194304 | tf_op jit(solution)/shard_map/psum | solution.py:34
  234.2 332.7 %all-reduce.8.cloned.1.call-start = ((), (), s32[]{:S(2)}) async-start(), calls=%async_computation.2 | async-start | bytes 4194304 | tf_op jit(solution)/shard_map/psum | solution.py:34
  412.5 5.6 copy-start.2
  412.5 5.6 copy-start.7
  569.4 1.4 copy-start
Sparse Core Ops, SparseCore 0:
  43.6 155.7 all-reduce.3
  234.3 148.7 all-reduce.5
  418.2 148.6 all-reduce.7
where the time goes:
time: 752 us; the launch traced here: 751 us
  waiting for transfers between devices  445 us (59%)
  blocking collectives  218 us (29%)
  local copies, waits for them, and re-layouts  38.6 us (5%)
  matrix products  30.4 us (4%)
  between operations  14.5 us (2%)
    psum x3, waiting for transfers between devices, residual_of(): pred = lax.psum(partial_value, 'var')  445 us
    psum x1, blocking collectives, body(): loss_total, pen_total = lax.psum((loss_part, pen_part), ('ind', 'var'))  74.1 us
    pmax x1, blocking collectives, body(): max_violation = lax.pmax(local_worst, 'var')  71.5 us
    psum x2, blocking collectives, body(): grad = lax.psum(partial_grad, 'ind') / total_rows  47.2 us
    psum x1, blocking collectives, body(): kkt_grad = lax.psum(kkt_partial, 'ind') / total_rows  24.8 us
    gather x1, local copies, waits for them, and re-layouts, body(): screened = jnp.take(dosages, screen_ids[0, :cap], axis=1)  17.2 us
    dot_general x3, matrix products, residual_of(): lax.dot_general(current.astype(jnp.bfloat16), screened, (((1,), (1,)), ((...  17 us
  transfers between devices with their start and end apart: 3, of which 3 were waited for; matrix products, arithmetic and copies ran while one was open for 1% of the time, Pallas kernels for 0%

commit v1 on v0

v1 whole, which is shorter than its diff:
```python
import functools

import jax
import jax.numpy as jnp
from jax import lax
from jax.experimental import pallas as pl
from jax.experimental.pallas import tpu as pltpu
from jax.sharding import PartitionSpec as P

MESH = pl.DeviceIdType.MESH
SWEEPS = 2
ROUNDS = SWEEPS + 1
NY, NZ = 4, 8
NIND = 8
CHUNKS = 4
NT = (((1,), (1,)), ((), ()))
Y_ORDER = (2, 1, 3)
Z_ORDER = (4, 3, 5, 2, 6, 1, 7)
ORDER = sorted(
    ((phase, chunk) for phase in range(1, 6) for chunk in range(CHUNKS)),
    key=lambda step: (step[1] + (0, 0, 1.5, 3, 4.5, 6)[step[0]], -step[0]),
)


def dot(a, b, **options):
    return jnp.dot(a, b, preferred_element_type=jnp.float32, **options)


def kernel(
    total_rows,
    dosages, phenotypes, screen_ids, screen_counts, kkt_ids, coef_prev, coef_slope, penalty,
    coef_out, resid_out, kkt_out, small_out,
    x, phen, psend, yrecv, zsend, zown, zrecv, gathered, isend, irecv, fsend, frecv, fz, fzrecv,
    x_sem, phen_sem, y_s, y_r, z_s, z_r, gz_s, gz_r, gy_s, gy_r, i_s, i_r, f_s, f_r,
):
    ind = lax.axis_index("ind")
    var = lax.axis_index("var")
    z, y = var // NY, lax.rem(var, NY)
    k, cap = coef_prev.shape
    width = x.shape[3]
    pool = x.shape[4]
    share = CHUNKS * width

    def at_y(step):
        return lax.rem(y + step, NY)

    def at_z(step):
        return lax.rem(z + step, NZ)

    def y_peer(step):
        return (ind, z * NY + at_y(step))

    def z_peer(step):
        return (ind, at_z(step) * NY + y)

    def i_peer(step):
        return (lax.rem(ind + step, NIND), var)

    x_copies = [
        pltpu.make_async_copy(dosages.at[:, :, c], x.at[c], x_sem.at[c]) for c in range(CHUNKS)
    ]
    for copy in x_copies:
        copy.start()
    phen_copy = pltpu.make_async_copy(
        phenotypes.at[:, pl.ds(pl.multiple_of(var * share, share), share)], phen, phen_sem
    )
    phen_copy.start()

    barrier = pltpu.get_barrier_semaphore()
    for step in range(1, NY):
        pl.semaphore_signal(barrier, inc=1, device_id=y_peer(step), device_id_type=MESH)
    for step in range(1, NZ):
        pl.semaphore_signal(barrier, inc=1, device_id=z_peer(step), device_id_type=MESH)
    for step in range(1, NIND):
        pl.semaphore_signal(barrier, inc=1, device_id=i_peer(step), device_id_type=MESH)

    live = (lax.broadcasted_iota(jnp.int32, (1, cap), 1) < screen_counts[0]).astype(jnp.float32)
    spread = (lax.broadcasted_iota(jnp.int32, (pool, cap), 0) == screen_ids[:, :cap]).astype(jnp.float32)
    batch = kkt_ids.shape[1]
    pick = (lax.broadcasted_iota(jnp.int32, (pool, batch), 0) == kkt_ids[...]).astype(jnp.float32)
    diagonal = lax.broadcasted_iota(jnp.int32, (k, k), 0) == lax.broadcasted_iota(jnp.int32, (k, k), 1)
    pen = jnp.sum(jnp.where(diagonal, jnp.broadcast_to(penalty[...], (k, k)), 0.0), axis=1, keepdims=True)
    shrink = 0.25 * pen
    ridge = 1.0 + 0.25 * pen
    exact = dict(preferred_element_type=jnp.float32, precision=lax.Precision.HIGHEST)
    warm = live * (coef_prev[...] + 0.5 * coef_slope[...])
    coef = lax.dot_general(warm, spread, NT, **exact)
    live_col = lax.dot_general(jnp.broadcast_to(live, (k, cap)), spread, NT, **exact)

    def remote(src, dst, send, recv, device):
        return pltpu.make_async_remote_copy(
            src_ref=src, dst_ref=dst, send_sem=send, recv_sem=recv, device_id=device, device_id_type=MESH
        )

    def drain(ref, sem):
        pltpu.make_async_copy(ref, ref, sem).wait()

    for r in range(ROUNDS):
        coef_bf = coef.astype(jnp.bfloat16)
        total = jnp.zeros((k, pool), jnp.float32)
        squares = jnp.zeros((k, 128), jnp.float32)
        for phase, c in ORDER:
            if phase == 1:
                if r == 0:
                    x_copies[c].wait()
                for step in Y_ORDER + (0,):
                    to = at_y(step)
                    for t in range(NZ):
                        psend[c, to, t] = lax.dot_general(
                            coef_bf, x[c, t, to], NT, preferred_element_type=jnp.float32
                        ).astype(jnp.bfloat16)
                    if r == 0 and c == 0 and step == Y_ORDER[0]:
                        pl.semaphore_wait(barrier, NY + NZ + NIND - 3)
                    if step:
                        remote(
                            psend.at[c, to], yrecv.at[r, c, step - 1], y_s.at[r, c], y_r.at[r, c], y_peer(step)
                        ).start()
            elif phase == 2:
                drain(yrecv.at[r, c], y_r.at[r, c])
                for step in Z_ORDER + (0,):
                    to = at_z(step)
                    part = psend[c, y, to].astype(jnp.float32)
                    for s in range(NY - 1):
                        part = part + yrecv[r, c, s, to].astype(jnp.float32)
                    if step:
                        zsend[c, to] = part.astype(jnp.bfloat16)
                        remote(
                            zsend.at[c, to], zrecv.at[r, c, step - 1], z_s.at[r, c], z_r.at[r, c], z_peer(step)
                        ).start()
                    else:
                        zown[c] = part
            elif phase == 3:
                drain(zrecv.at[r, c], z_r.at[r, c])
                if r == 0 and c == 0:
                    phen_copy.wait()
                pred = zown[c]
                for s in range(NZ - 1):
                    pred = pred + zrecv[r, c, s].astype(jnp.float32)
                columns = slice(c * width, (c + 1) * width)
                resid = phen[:, columns] - pred
                if r == ROUNDS - 1:
                    resid_out[:, columns] = resid
                gathered[r, c, y, z] = resid.astype(jnp.bfloat16)
                for step in Z_ORDER:
                    block = gathered.at[r, c, y, z]
                    remote(block, block, gz_s.at[r, c], gz_r.at[r, c], z_peer(step)).start()
            else:
                if phase == 4:
                    drain(gathered.at[r, c, y, pl.ds(0, NZ - 1)], gz_r.at[r, c])
                    for step in Y_ORDER:
                        blocks = gathered.at[r, c, y]
                        remote(blocks, blocks, gy_s.at[r, c], gy_r.at[r, c], y_peer(step)).start()
                else:
                    drain(gathered.at[r, c, pl.ds(0, NY - 1)], gy_r.at[r, c])
                for step in (0,) if phase == 4 else (1, 2, 3):
                    of = at_y(step)
                    for t in range(NZ):
                        block = gathered[r, c, of, t]
                        total = total + dot(block, x[c, t, of])
                        if r == ROUNDS - 1:
                            wide = block.astype(jnp.float32)
                            for lane in range(0, width, 128):
                                piece = wide[:, lane:lane + 128]
                                squares = squares + piece * piece
        last = r == ROUNDS - 1
        if last:
            loss = jnp.sum(squares, axis=1, keepdims=True)
            kkt_part = dot(total, pick, precision=lax.Precision.HIGHEST)
            total = jnp.concatenate([kkt_part, jnp.broadcast_to(loss, (k, 128 - batch))], axis=1)
            isend[r, :, :128] = total
            dst = irecv.at[r, :, :, pl.ds(0, 128)]
            src = isend.at[r, :, pl.ds(0, 128)]
        else:
            isend[r] = total
            dst = irecv.at[r]
            src = isend.at[r]
        for step in range(1, NIND):
            remote(src, dst.at[ind], i_s.at[r], i_r.at[r], i_peer(step)).start()
        if last:
            irecv[r, ind, :, :128] = total
        else:
            irecv[r, ind] = total
        for c in range(CHUNKS):
            drain(yrecv.at[r, c], y_s.at[r, c])
            drain(zrecv.at[r, c], z_s.at[r, c])
            drain(zrecv.at[r, c], gz_s.at[r, c])
            drain(yrecv.at[r, c], gy_s.at[r, c])
        others = dst.at[pl.ds(0, NIND - 1)]
        drain(others, i_r.at[r])
        total = irecv[r, 0, :, :128] if last else irecv[r, 0]
        for s in range(1, NIND):
            total = total + (irecv[r, s, :, :128] if last else irecv[r, s])
        drain(others, i_s.at[r])
        if not last:
            moved = coef + 0.5 * (total / total_rows)
            coef = live_col * (jnp.maximum(moved - shrink, 0.0) + jnp.minimum(moved + shrink, 0.0)) / ridge

    kkt_grad = total[:, :batch] / total_rows
    kkt_out[...] = kkt_grad
    loss = total[:, batch:batch + 1] / (2.0 * total_rows)
    worst = jnp.max(jnp.maximum(jnp.abs(kkt_grad) - 0.5 * pen, 0.0), axis=1, keepdims=True)
    pen_part = pen * jnp.sum(0.5 * jnp.abs(coef) + 0.25 * coef * coef, axis=1, keepdims=True)

    rows = lax.broadcasted_iota(jnp.int32, (k, 128), 0)
    lanes = lax.broadcasted_iota(jnp.int32, (k, 128), 1)

    def as_row(column):
        return jnp.sum(jnp.where(rows == lanes, column, 0.0), axis=0, keepdims=True)

    upper = lax.broadcasted_iota(jnp.int32, (8, 128), 0) == 0
    fsend[...] = jnp.where(upper, as_row(worst), as_row(pen_part))

    def merge(a, b):
        return jnp.where(upper, jnp.maximum(a, b), a + b)

    for step in Y_ORDER:
        remote(fsend, frecv.at[y], f_s.at[0], f_r.at[0], y_peer(step)).start()
    frecv[y] = fsend[...]
    coef_out[...] = dot(coef, spread, precision=lax.Precision.HIGHEST)
    drain(frecv.at[pl.ds(0, NY - 1)], f_r.at[0])
    both = frecv[0]
    for s in range(1, NY):
        both = merge(both, frecv[s])
    fz[...] = both
    for step in Z_ORDER:
        remote(fz, fzrecv.at[z], f_s.at[1], f_r.at[1], z_peer(step)).start()
    fzrecv[z] = both
    drain(fzrecv.at[pl.ds(0, NZ - 1)], f_r.at[1])
    both = fzrecv[0]
    for s in range(1, NZ):
        both = merge(both, fzrecv[s])
    small_out[...] = jnp.where(upper, both, both + as_row(loss))
    drain(frecv.at[pl.ds(0, NY - 1)], f_s.at[0])
    drain(fzrecv.at[pl.ds(0, NZ - 1)], f_s.at[1])


def body(dosages, phenotypes, screen_ids, screen_counts, kkt_ids, coef_prev, coef_slope, penalty):
    row_dev, pool = dosages.shape
    k, cap = coef_prev.shape
    batch = kkt_ids.shape[1]
    n_var = lax.axis_size("var")
    share = row_dev // n_var
    width = share // CHUNKS
    bf, f32 = jnp.bfloat16, jnp.float32
    vmem = pl.BlockSpec(memory_space=pltpu.VMEM)
    hbm = pl.BlockSpec(memory_space=pl.ANY)
    smem = pl.BlockSpec(memory_space=pltpu.SMEM)
    dma = pltpu.SemaphoreType.DMA
    coef, resid, kkt, small = pl.pallas_call(
        functools.partial(kernel, row_dev * lax.axis_size("ind")),
        out_shape=(
            jax.ShapeDtypeStruct((k, cap), f32),
            jax.ShapeDtypeStruct((k, share), f32),
            jax.ShapeDtypeStruct((k, batch), f32),
            jax.ShapeDtypeStruct((8, 128), f32),
        ),
        in_specs=[hbm, hbm, vmem, smem, vmem, vmem, vmem, vmem],
        out_specs=(vmem, vmem, vmem, vmem),
        scratch_shapes=[
            pltpu.VMEM((CHUNKS, NZ, NY, width, pool), bf),
            pltpu.VMEM((k, share), f32),
            pltpu.VMEM((CHUNKS, NY, NZ, k, width), bf),
            pltpu.VMEM((ROUNDS, CHUNKS, NY - 1, NZ, k, width), bf),
            pltpu.VMEM((CHUNKS, NZ, k, width), bf),
            pltpu.VMEM((CHUNKS, k, width), f32),
            pltpu.VMEM((ROUNDS, CHUNKS, NZ - 1, k, width), bf),
            pltpu.VMEM((ROUNDS, CHUNKS, NY, NZ, k, width), bf),
            pltpu.VMEM((ROUNDS, k, pool), f32),
            pltpu.VMEM((ROUNDS, NIND, k, pool), f32),
            pltpu.VMEM((8, 128), f32),
            pltpu.VMEM((NY, 8, 128), f32),
            pltpu.VMEM((8, 128), f32),
            pltpu.VMEM((NZ, 8, 128), f32),
            dma((CHUNKS,)),
            dma,
        ] + [dma((ROUNDS, CHUNKS))] * 8 + [dma((ROUNDS,))] * 2 + [dma((2,))] * 2,
        compiler_params=pltpu.CompilerParams(
            collective_id=0, has_side_effects=True, vmem_limit_bytes=48 * 1024 * 1024
        ),
        cost_estimate=pl.CostEstimate(
            flops=2 * 2 * ROUNDS * k * pool * row_dev, bytes_accessed=2 * pool * row_dev, transcendentals=0
        ),
        name="elastic_net_step",
    )(
        dosages.reshape(NZ, NY, CHUNKS, width, pool),
        phenotypes, screen_ids, screen_counts, kkt_ids, coef_prev, coef_slope, penalty.reshape(1, k),
    )
    return (coef, resid, kkt, small[0, :k], small[1, :k])


def solution(mesh):
    placed = (
        P("ind", "var"),
        P(None, "ind"),
        P("var", None),
        P("var"),
        P("var", None),
        P(None, "var"),
        P(None, "var"),
        P(),
    )
    return jax.shard_map(
        body,
        mesh=mesh,
        in_specs=placed,
        out_specs=(P(None, "var"), P(None, ("ind", "var")), P(None, "var"), P(), P()),
        check_vma=False,
    )
```

time: 752 us -> 136 us (0.18)
  waiting for transfers between devices: 445 us -> 0 us
  blocking collectives: 218 us -> 0 us
  Pallas kernels: 0 us -> 126 us
  local copies, waits for them, and re-layouts: 38.6 us -> 7.45 us
  matrix products: 30.4 us -> 0 us
  between operations: 14.5 us -> 1.3 us
    psum x3 -> x0, waiting for transfers between devices: 445 us -> none  [residual_of(): pred = lax.psum(partial_value, 'var')]
    psum x4 -> x0, blocking collectives: 146 us -> none  [the longest x1 74.1 us: body(): loss_total, pen_total = lax.psum((loss_part, pen_part), ('ind', 'var'))]
    pallas_call x0 -> x1, Pallas kernels: none -> 126 us  [body(): pl.pallas_call(functools.partial(kernel, row_dev * lax.axis_size('ind')),...]
    pmax x1 -> x0, blocking collectives: 71.5 us -> none  [body(): max_violation = lax.pmax(local_worst, 'var')]
    dot_general x6 -> x0, matrix products: 30.4 us -> none  [the longest x3 17 us: residual_of(): lax.dot_general(current.astype(jnp.bfloat16), screened, (((1,), (1,)), ((...]
    gather x2 -> x0, local copies, waits for them, and re-layouts: 25.3 us -> none  [the longest x1 17.2 us: body(): screened = jnp.take(dosages, screen_ids[0, :cap], axis=1)]
  transfers between devices with their start and end apart: 3 -> 0, of which waited for: 3 -> 0; matrix products, arithmetic and copies ran while one was open for 1% -> 0% of each run, Pallas kernels for 0% -> 0%
where the time goes in v1:
time: 136 us; the launch traced here: 135 us
  Pallas kernels  126 us (93%)
  local copies, waits for them, and re-layouts  7.45 us (5%)
    pallas_call x1, Pallas kernels, body(): pl.pallas_call(functools.partial(kernel, row_dev * lax.axis_size('ind')),...  126 us
    unnamed x15, local copies, waits for them, and re-layouts  6.94 us

profile of v1, /device:TPU:8, one launch (start us, length us, event | category | flops | bytes accessed | tf_op | source)
XLA Modules:
  0.0 135.0 jit_solution(12070103474951655738)
XLA Ops:
  1.3 0.0 copy-start
  1.3 1.6 %copy-done = f32[32,16384]{1,0:T(8,128)S(1)} copy-done((f32[32,16384]{1,0:T(8,128)S(1)}, f32[32,16384]{1,0:T(8,128)}, u32[]{:S(2)}) %copy-start) | copy-done | bytes 2097176
  2.9 0.0 copy-start.1
  2.9 0.8 copy-done.1
  3.6 0.0 copy-start.2
  3.6 0.8 copy-done.2
  4.4 0.0 copy-start.3
  4.4 0.7 copy-done.3
  5.1 0.0 copy-start.4
  5.1 0.7 copy-done.4
  5.7 0.0 copy-start.5
  5.7 0.7 copy-done.5
  6.4 126.3 %elastic_net_step.1 = (f32[32,192]{1,0:T(8,128)S(1)}, f32[32,512]{1,0:T(8,128)S(1)}, f32[32,64]{1,0:T(8,128)S(1)}, f32[8,128]{1,0:T(8,128)S(1)}) custom-call(bf16[8,4,4,128,256]{4,3,2,1,0:T(8,128)(2,1)} %bitcast.7, f32[32,16384]{1,0:T(8,128)S(1)} %copy-done, s32[1,256]{1,0:T(1,128)S(1)} %copy-done.3, s32[1]{0:T(128)S(6)} %copy.16.screen_counts, ...), custom_call_target="tpu_custom_call" | custom-call | flops 1610612736 | bytes 8388608 | tf_op jit(solution)/shard_map/elastic_net_step/pallas_call | solution.py:249
  132.7 0.5 slice_bitcast_fusion
  133.2 0.6 copy.17
  133.8 0.6 copy.18
  134.4 0.6 copy.19
Async XLA Ops:
  1.3 1.6 %copy-start = (f32[32,16384]{1,0:T(8,128)S(1)}, f32[32,16384]{1,0:T(8,128)}, u32[]{:S(2)}) copy-start(f32[32,16384]{1,0:T(8,128)} %phenotypes.1) | copy-start | bytes 6291460
  2.9 0.8 copy-start.1
  3.6 0.8 copy-start.2
  4.4 0.7 copy-start.3
  5.1 0.7 copy-start.4
  5.7 0.7 copy-start.5

commit v2 on v0

v2 whole, which is shorter than its diff:
```python
import functools

import jax
import jax.numpy as jnp
from jax import lax
from jax.experimental import pallas as pl
from jax.experimental.pallas import tpu as pltpu
from jax.sharding import PartitionSpec as P

MESH = pl.DeviceIdType.MESH
SWEEPS = 2
ROUNDS = SWEEPS + 1
NY, NZ = 4, 8
NIND = 8
CHUNKS = 2
GROUPS = 2
NT = (((1,), (1,)), ((), ()))
Z_ORDER = (4, 3, 5, 2, 6, 1, 7)
EXACT = dict(preferred_element_type=jnp.float32, precision=lax.Precision.HIGHEST)
BF, F32 = jnp.bfloat16, jnp.float32

PERIOD, STAGGER, SPACING = 26.0, 8.0, 2.0
OFFSET = {1: 0.0, 2: 5.0, 3: 9.5, 4: 14.0, 5: 18.5, 6: 25.0}


def nominal(step):
    group, r, phase, c = step
    return group * STAGGER + r * PERIOD + OFFSET[phase] + c * (0.6 if phase == 1 else SPACING)


ORDER = [(0, 0, 1, 0), (0, 0, 1, 1), (1, 0, 1, 0), (0, 0, 2, 0), (1, 0, 1, 1), (0, 0, 2, 1), (0, 0, 3, 0), (1, 0, 2, 0), (0, 0, 3, 1), (0, 0, 4, 0), (1, 0, 2, 1), (1, 0, 3, 0), (0, 0, 4, 1), (1, 0, 3, 1), (1, 0, 4, 0), (0, 0, 5, 0), (0, 0, 5, 1), (1, 0, 4, 1), (1, 0, 5, 0), (0, 0, 6, 0), (0, 1, 1, 0), (1, 0, 5, 1), (0, 1, 1, 1), (0, 1, 2, 0), (1, 0, 6, 0), (1, 1, 1, 0), (0, 1, 2, 1), (1, 1, 1, 1), (0, 1, 3, 0), (1, 1, 2, 0), (0, 1, 3, 1), (0, 1, 4, 0), (1, 1, 2, 1), (1, 1, 3, 0), (0, 1, 4, 1), (1, 1, 3, 1), (1, 1, 4, 0), (0, 1, 5, 0), (0, 1, 5, 1), (1, 1, 4, 1), (1, 1, 5, 0), (0, 1, 6, 0), (0, 2, 1, 0), (1, 1, 5, 1), (0, 2, 1, 1), (0, 2, 2, 0), (1, 1, 6, 0), (1, 2, 1, 0), (0, 2, 2, 1), (1, 2, 1, 1), (0, 2, 3, 0), (1, 2, 2, 0), (0, 2, 3, 1), (1, 2, 2, 1), (0, 2, 4, 0), (1, 2, 3, 0), (0, 2, 4, 1), (1, 2, 3, 1), (1, 2, 4, 0), (0, 2, 5, 0), (1, 2, 4, 1), (0, 2, 5, 1), (1, 2, 5, 0), (1, 2, 5, 1), (0, 2, 6, 0), (1, 2, 6, 0)]


def kernel(
    total_rows,
    dosages, phenotypes, screen_ids, screen_counts, kkt_ids, coef_prev, coef_slope, penalty,
    coef_hbm, resid_hbm, kkt_hbm, worst_hbm, objective_hbm,
    coef_out, resid_out, kkt_out, worst_out, objective_out, x, phen, ids_v, counts_s, kkt_v, prev_v, slope_v, pen_v,
    psend, yown, yrecv, zsend, zown, zrecv, gathered, irecv, lrecv, frecv, fzrecv,
    x_sem, in_sem, out_sem, y_s, y_r, z_s, z_r, gz_s, gz_r, gy_s, gy_r, i_s, i_r, f_s, f_r,
):
    ind = lax.axis_index("ind")
    var = lax.axis_index("var")
    z, y = var // NY, lax.rem(var, NY)
    k, cap = prev_v.shape
    width, pool = x.shape[3:]
    share = CHUNKS * width
    kg = k // GROUPS
    batch = kkt_v.shape[1]

    def at_y(step):
        return lax.rem(y + step, NY)

    def at_z(step):
        return lax.rem(z + step, NZ)

    def y_peer(step):
        return (ind, z * NY + at_y(step))

    def z_peer(step):
        return (ind, at_z(step) * NY + y)

    def i_peer(step):
        return (lax.rem(ind + step, NIND), var)

    small = [
        pltpu.make_async_copy(src, dst, in_sem.at[n])
        for n, (src, dst) in enumerate((
            (screen_ids, ids_v), (screen_counts, counts_s), (kkt_ids, kkt_v),
            (coef_prev, prev_v), (coef_slope, slope_v), (penalty, pen_v),
        ))
    ]
    phen_copy = pltpu.make_async_copy(
        phenotypes.at[:, pl.ds(pl.multiple_of(var * share, share), share)], phen, in_sem.at[len(small)]
    )
    x_copies = [pltpu.make_async_copy(dosages.at[:, :, c], x.at[c], x_sem.at[c]) for c in range(CHUNKS)]
    for copy in small + x_copies + [phen_copy]:
        copy.start()

    barrier = pltpu.get_barrier_semaphore()
    for step in range(1, NY):
        pl.semaphore_signal(barrier, inc=1, device_id=y_peer(step), device_id_type=MESH)
    for step in range(1, NZ):
        pl.semaphore_signal(barrier, inc=1, device_id=z_peer(step), device_id_type=MESH)
    for step in range(1, NIND):
        pl.semaphore_signal(barrier, inc=1, device_id=i_peer(step), device_id_type=MESH)

    for copy in small:
        copy.wait()
    live = (lax.broadcasted_iota(jnp.int32, (1, cap), 1) < counts_s[...]).astype(F32)
    spread = (lax.broadcasted_iota(jnp.int32, (pool, cap), 0) == ids_v[:, :cap]).astype(F32)
    pick = (lax.broadcasted_iota(jnp.int32, (pool, batch), 0) == kkt_v[...]).astype(F32)
    diagonal = lax.broadcasted_iota(jnp.int32, (k, k), 0) == lax.broadcasted_iota(jnp.int32, (k, k), 1)
    pen_all = jnp.sum(jnp.where(diagonal, jnp.broadcast_to(pen_v[...], (k, k)), 0.0), axis=1, keepdims=True)
    warm = lax.dot_general(live * (prev_v[...] + 0.5 * slope_v[...]), spread, NT, **EXACT)
    live_col = lax.dot_general(jnp.broadcast_to(live, (kg, cap)), spread, NT, **EXACT)
    members = [slice(g * kg, (g + 1) * kg) for g in range(GROUPS)]
    pens = [pen_all[rows] for rows in members]
    coefs = [warm[rows] for rows in members]
    totals = [None] * GROUPS
    squares = [jnp.zeros((kg, 128), F32)] * GROUPS
    worsts, losses = [None] * GROUPS, [None] * GROUPS

    def remote(src, dst, send, recv, device):
        return pltpu.make_async_remote_copy(
            src_ref=src, dst_ref=dst, send_sem=send, recv_sem=recv, device_id=device, device_id_type=MESH
        )

    written = 0
    puts = []

    def put(src, dst, slot):
        puts.append(pltpu.make_async_copy(src, dst, out_sem.at[slot]))
        puts[-1].start()

    def drain(ref, sem):
        pltpu.make_async_copy(ref, ref, sem).wait()

    def three(g, r, c):
        return gathered.at[r, g, c, pl.ds(0, NY - 1)]

    def seven(g, r, c):
        return gathered.at[r, g, c, 0, pl.ds(0, NZ - 1)]

    for g, r, phase, c in ORDER:
        here = (r, g, c)
        last = r == ROUNDS - 1
        if phase == 1:
            if x_copies[c] is not None:
                x_copies[c].wait()
                x_copies[c] = None
            if r > 0:
                drain(three(g, r, c), y_s.at[r - 1, g, c])
            coef_bf = coefs[g].astype(BF)

            def predict(to):
                for t in range(NZ):
                    psend[g, c, to, t] = lax.dot_general(
                        coef_bf, x[c, t, to], NT, preferred_element_type=F32
                    ).astype(BF)

            @pl.loop(1, NY)
            def _(step):
                to = at_y(step)
                predict(to)
                if (g, r, phase, c) == ORDER[0]:
                    @pl.when(step == 1)
                    def _():
                        pl.semaphore_wait(barrier, NY + NZ + NIND - 3)
                remote(psend.at[g, c, to], yrecv.at[r, g, c, step - 1], y_s.at[here], y_r.at[here], y_peer(step)).start()

            for t in range(NZ):
                yown[g, c, t] = lax.dot_general(coef_bf, x[c, t, y], NT, preferred_element_type=F32)
        elif phase == 2:
            if r > 0:
                drain(seven(g, r, c), z_s.at[r - 1, g, c])
            drain(three(g, r, c), y_r.at[here])
            for step in Z_ORDER + (0,):
                to = at_z(step)
                part = yown[g, c, to]
                for s in range(NY - 1):
                    part = part + yrecv[r, g, c, s, to].astype(F32)
                if step:
                    zsend[g, c, to] = part.astype(BF)
                    remote(zsend.at[g, c, to], zrecv.at[r, g, c, step - 1], z_s.at[here], z_r.at[here], z_peer(step)).start()
                else:
                    zown[g, c] = part
        elif phase == 3:
            drain(seven(g, r, c), z_r.at[here])
            if phen_copy is not None:
                phen_copy.wait()
                phen_copy = None
            pred = zown[g, c]
            for s in range(NZ - 1):
                pred = pred + zrecv[r, g, c, s].astype(F32)
            columns = slice(c * width, (c + 1) * width)
            resid = phen[members[g], columns] - pred
            if last:
                resid_out[members[g], columns] = resid
                written += 1
                if written == GROUPS * CHUNKS:
                    put(resid_out, resid_hbm, 0)
            gathered[r, g, c, y, z] = resid.astype(BF)
            block = gathered.at[r, g, c, y, z]
            for step in Z_ORDER:
                remote(block, block, gz_s.at[here], gz_r.at[here], z_peer(step)).start()
        elif phase in (4, 5):
            if phase == 4:
                drain(seven(g, r, c), gz_r.at[here])
                blocks = gathered.at[r, g, c, y]
                for step in (2, 1, 3):
                    remote(blocks, blocks, gy_s.at[here], gy_r.at[here], y_peer(step)).start()
            else:
                drain(three(g, r, c), gy_r.at[here])

            def contract(of, carry):
                total, square = carry
                for t in range(NZ):
                    block = gathered[r, g, c, of, t]
                    total = total + jnp.dot(block, x[c, t, of], preferred_element_type=F32)
                    if last:
                        wide = block.astype(F32)
                        for lane in range(0, width, 128):
                            square = square + wide[:, lane:lane + 128] * wide[:, lane:lane + 128]
                return total, square

            if phase == 4:
                if c == 0:
                    totals[g] = jnp.zeros((kg, pool), F32)
                carry = contract(y, (totals[g], squares[g]))
            else:
                carry = lax.fori_loop(1, NY, lambda step, carry: contract(at_y(step), carry), (totals[g], squares[g]))
            totals[g], squares[g] = carry
            if phase == 5 and c == CHUNKS - 1:
                if last:
                    loss = jnp.sum(squares[g], axis=1, keepdims=True)
                    kkt_part = jnp.dot(totals[g], pick, **EXACT)
                    lrecv[g, ind] = jnp.concatenate([kkt_part, jnp.broadcast_to(loss, (kg, 128 - batch))], axis=1)
                    slot = lrecv.at[g, ind]
                else:
                    irecv[r, g, ind] = totals[g]
                    slot = irecv.at[r, g, ind]
                for step in (4, 5, 2, 3, 6, 7, 1):
                    remote(slot, slot, i_s.at[r, g], i_r.at[r, g], i_peer(step)).start()
        elif not last:
            drain(irecv.at[r, g, pl.ds(0, NIND - 1)], i_r.at[r, g])
            total = irecv[r, g, 0]
            for s in range(1, NIND):
                total = total + irecv[r, g, s]
            moved = coefs[g] + 0.5 * (total / total_rows)
            shrink = 0.25 * pens[g]
            soft = jnp.maximum(moved - shrink, 0.0) + jnp.minimum(moved + shrink, 0.0)
            coefs[g] = live_col * soft / (1.0 + 0.25 * pens[g])
        else:
            drain(lrecv.at[g, pl.ds(0, NIND - 1)], i_r.at[r, g])
            total = lrecv[g, 0]
            for s in range(1, NIND):
                total = total + lrecv[g, s]
            kkt_grad = total[:, :batch] / total_rows
            kkt_out[members[g]] = kkt_grad
            losses[g] = total[:, batch:batch + 1] / (2.0 * total_rows)
            worsts[g] = jnp.max(jnp.maximum(jnp.abs(kkt_grad) - 0.5 * pens[g], 0.0), axis=1, keepdims=True)

    lanes = lax.broadcasted_iota(jnp.int32, (kg, 128), 1)
    rows = lax.broadcasted_iota(jnp.int32, (kg, 128), 0)

    def as_row(columns):
        return sum(
            jnp.sum(jnp.where(rows + g * kg == lanes, columns[g], 0.0), axis=0, keepdims=True) for g in range(GROUPS)
        )

    pen_part = [
        pens[g] * jnp.sum(0.5 * jnp.abs(coefs[g]) + 0.25 * coefs[g] * coefs[g], axis=1, keepdims=True)
        for g in range(GROUPS)
    ]
    upper = lax.broadcasted_iota(jnp.int32, (8, 128), 0) == 0

    def merge(a, b):
        return jnp.where(upper, jnp.maximum(a, b), a + b)

    frecv[y] = jnp.where(upper, as_row(worsts), as_row(pen_part))
    for step in (2, 1, 3):
        remote(frecv.at[y], frecv.at[y], f_s.at[0], f_r.at[0], y_peer(step)).start()
    for g in range(GROUPS):
        coef_out[members[g]] = jnp.dot(coefs[g], spread, **EXACT)
    put(coef_out, coef_hbm, 1)
    put(kkt_out, kkt_hbm, 2)
    drain(frecv.at[pl.ds(0, NY - 1)], f_r.at[0])
    both = frecv[0]
    for s in range(1, NY):
        both = merge(both, frecv[s])
    fzrecv[z] = both
    for step in Z_ORDER:
        remote(fzrecv.at[z], fzrecv.at[z], f_s.at[1], f_r.at[1], z_peer(step)).start()
    end = ROUNDS - 1
    for g in range(GROUPS):
        for c in range(CHUNKS):
            drain(three(g, end, c), y_s.at[end, g, c])
            drain(seven(g, end, c), z_s.at[end, g, c])
            for r in range(ROUNDS):
                drain(seven(g, r, c), gz_s.at[r, g, c])
                drain(three(g, r, c), gy_s.at[r, g, c])
        for r in range(end):
            drain(irecv.at[r, g, pl.ds(0, NIND - 1)], i_s.at[r, g])
        drain(lrecv.at[g, pl.ds(0, NIND - 1)], i_s.at[end, g])
    drain(frecv.at[pl.ds(0, NY - 1)], f_s.at[0])
    drain(fzrecv.at[pl.ds(0, NZ - 1)], f_r.at[1])
    both = fzrecv[0]
    for s in range(1, NZ):
        both = merge(both, fzrecv[s])
    worst_out[...] = both[:1, :k]
    objective_out[...] = (both[1:2] + as_row(losses))[:, :k]
    put(worst_out, worst_hbm, 3)
    put(objective_out, objective_hbm, 4)
    drain(fzrecv.at[pl.ds(0, NZ - 1)], f_s.at[1])
    for copy in puts:
        copy.wait()


def hand_over(*refs):
    n = len(refs) // 2
    for source, target in zip(refs[:n], refs[n:]):
        target[...] = source[...]


def body(dosages, phenotypes, screen_ids, screen_counts, kkt_ids, coef_prev, coef_slope, penalty):
    row_dev, pool = dosages.shape
    k, cap = coef_prev.shape
    batch = kkt_ids.shape[1]
    share = row_dev // lax.axis_size("var")
    width = share // CHUNKS
    kg = k // GROUPS
    hbm = pl.BlockSpec(memory_space=pl.ANY)
    dma = pltpu.SemaphoreType.DMA
    each = (ROUNDS, GROUPS, CHUNKS)
    shapes = [(k, cap), (k, share), (k, batch), (1, k), (1, k)]
    results = pl.pallas_call(
        functools.partial(kernel, row_dev * lax.axis_size("ind")),
        out_shape=[jax.ShapeDtypeStruct(shape, F32) for shape in shapes],
        in_specs=[hbm] * 8,
        out_specs=[hbm] * 5,
        scratch_shapes=[
            pltpu.VMEM((k, cap), F32),
            pltpu.VMEM((k, share), F32),
            pltpu.VMEM((k, batch), F32),
            pltpu.VMEM((1, k), F32),
            pltpu.VMEM((1, k), F32),
            pltpu.VMEM((CHUNKS, NZ, NY, width, pool), BF),
            pltpu.VMEM((k, share), F32),
            pltpu.VMEM(screen_ids.shape, jnp.int32),
            pltpu.VMEM((1, 1), jnp.int32),
            pltpu.VMEM(kkt_ids.shape, jnp.int32),
            pltpu.VMEM((k, cap), F32),
            pltpu.VMEM((k, cap), F32),
            pltpu.VMEM((1, k), F32),
            pltpu.VMEM((GROUPS, CHUNKS, NY, NZ, kg, width), BF),
            pltpu.VMEM((GROUPS, CHUNKS, NZ, kg, width), F32),
            pltpu.VMEM(each + (NY - 1, NZ, kg, width), BF),
            pltpu.VMEM((GROUPS, CHUNKS, NZ, kg, width), BF),
            pltpu.VMEM((GROUPS, CHUNKS, kg, width), F32),
            pltpu.VMEM(each + (NZ - 1, kg, width), BF),
            pltpu.VMEM(each + (NY, NZ, kg, width), BF),
            pltpu.VMEM((SWEEPS, GROUPS, NIND, kg, pool), F32),
            pltpu.VMEM((GROUPS, NIND, kg, 128), F32),
            pltpu.VMEM((NY, 8, 128), F32),
            pltpu.VMEM((NZ, 8, 128), F32),
            dma((CHUNKS,)),
            dma((7,)),
            dma((5,)),
        ] + [dma(each)] * 8 + [dma((ROUNDS, GROUPS))] * 2 + [dma((2,))] * 2,
        compiler_params=pltpu.CompilerParams(
            collective_id=0, has_side_effects=True, vmem_limit_bytes=56 * 1024 * 1024
        ),
        cost_estimate=pl.CostEstimate(
            flops=2 * 2 * ROUNDS * k * pool * row_dev, bytes_accessed=2 * pool * row_dev, transcendentals=0
        ),
        name="elastic_net_step",
    )(
        dosages.reshape(NZ, NY, CHUNKS, width, pool),
        phenotypes, screen_ids, screen_counts.reshape(1, 1), kkt_ids, coef_prev, coef_slope, penalty.reshape(1, k),
    )
    coef, resid, kkt, worst, objective = pl.pallas_call(
        hand_over,
        out_shape=[jax.ShapeDtypeStruct(shape, F32) for shape in shapes],

        name="hand_over",
    )(*results)
    return (coef, resid, kkt, worst.reshape(k), objective.reshape(k))


def solution(mesh):
    placed = (
        P("ind", "var"),
        P(None, "ind"),
        P("var", None),
        P("var"),
        P("var", None),
        P(None, "var"),
        P(None, "var"),
        P(),
    )
    return jax.shard_map(
        body,
        mesh=mesh,
        in_specs=placed,
        out_specs=(P(None, "var"), P(None, ("ind", "var")), P(None, "var"), P(), P()),
        check_vma=False,
    )
```

time: 752 us -> 114 us (0.15)
  waiting for transfers between devices: 445 us -> 0 us
  blocking collectives: 218 us -> 0 us
  Pallas kernels: 0 us -> 112 us
  local copies, waits for them, and re-layouts: 38.6 us -> 0 us
  matrix products: 30.4 us -> 0 us
  between operations: 14.5 us -> 1.29 us
    psum x3 -> x0, waiting for transfers between devices: 445 us -> none  [residual_of(): pred = lax.psum(partial_value, 'var')]
    psum x4 -> x0, blocking collectives: 146 us -> none  [the longest x1 74.1 us: body(): loss_total, pen_total = lax.psum((loss_part, pen_part), ('ind', 'var'))]
    pallas_call x0 -> x2, Pallas kernels: none -> 112 us  [the longest x1 110 us: body(): pl.pallas_call(functools.partial(kernel, row_dev * lax.axis_size('ind')),...]
    pmax x1 -> x0, blocking collectives: 71.5 us -> none  [body(): max_violation = lax.pmax(local_worst, 'var')]
    dot_general x6 -> x0, matrix products: 30.4 us -> none  [the longest x3 17 us: residual_of(): lax.dot_general(current.astype(jnp.bfloat16), screened, (((1,), (1,)), ((...]
    gather x2 -> x0, local copies, waits for them, and re-layouts: 25.3 us -> none  [the longest x1 17.2 us: body(): screened = jnp.take(dosages, screen_ids[0, :cap], axis=1)]
    unnamed x17 -> x0, local copies, waits for them, and re-layouts: 13.3 us -> none
  transfers between devices with their start and end apart: 3 -> 0, of which waited for: 3 -> 0; matrix products, arithmetic and copies ran while one was open for 1% -> 0% of each run, Pallas kernels for 0% -> 0%
where the time goes in v2:
time: 114 us; the launch traced here: 113 us
  Pallas kernels  112 us (98%)
  between operations  1.29 us (1%)
    pallas_call x1, Pallas kernels, body(): pl.pallas_call(functools.partial(kernel, row_dev * lax.axis_size('ind')),...  110 us

profile of v2, /device:TPU:8, one launch (start us, length us, event | category | flops | bytes accessed | tf_op | source)
XLA Modules:
  0.0 113.3 jit_solution(14727854852933450008)
XLA Ops:
  1.3 110.5 %elastic_net_step.1 = (f32[32,192]{1,0:T(8,128)}, f32[32,512]{1,0:T(8,128)}, f32[32,64]{1,0:T(8,128)}, f32[1,32]{1,0:T(1,128)}, f32[1,32]{1,0:T(1,128)}) custom-call(bf16[8,4,2,256,256]{4,3,2,1,0:T(8,128)(2,1)} %bitcast.6, f32[32,16384]{1,0:T(8,128)} %phenotypes.1, s32[1,256]{1,0:T(1,128)} %screen_ids.1, s32[1,1]{1,0:T(1,128)} %bitcast.5.screen_counts, ...), custom_call_target="tpu_custom_call" | custom-call | flops 1610612736 | bytes 8388608 | tf_op jit(solution)/shard_map/elastic_net_step/pallas_call | solution.py:317
  111.8 1.5 %hand_over.1 = (f32[32,192]{1,0:T(8,128)}, f32[32,512]{1,0:T(8,128)}, f32[32,64]{1,0:T(8,128)}, f32[1,32]{1,0:T(1,128)}, f32[1,32]{1,0:T(1,128)}) custom-call(f32[32,192]{1,0:T(8,128)} %get-tuple-element.15.refs_0_, f32[32,512]{1,0:T(8,128)} %get-tuple-element.16.refs_1_, f32[32,64]{1,0:T(8,128)} %get-tuple-element.17.refs_2_, ...), custom_call_target="tpu_custom_call" | custom-call | tf_op jit(solution)/shard_map/hand_over/pallas_call | solution.py:362

commit v3 on v2

--- a/solution.py
+++ b/solution.py
@@ -139,14 +139,11 @@
                         coef_bf, x[c, t, to], NT, preferred_element_type=F32
                     ).astype(BF)
 
-            @pl.loop(1, NY)
-            def _(step):
+            for step in (1, 2, 3):
                 to = at_y(step)
                 predict(to)
-                if (g, r, phase, c) == ORDER[0]:
-                    @pl.when(step == 1)
-                    def _():
-                        pl.semaphore_wait(barrier, NY + NZ + NIND - 3)
+                if (g, r, phase, c, step) == ORDER[0] + (1,):
+                    pl.semaphore_wait(barrier, NY + NZ + NIND - 3)
                 remote(psend.at[g, c, to], yrecv.at[r, g, c, step - 1], y_s.at[here], y_r.at[here], y_peer(step)).start()
 
             for t in range(NZ):

time: 114 us -> 113 us (level)
  no operation moved by 1% of the time
where the time goes in v3:
time: 113 us
  Pallas kernels  111 us (98%)
  between operations  1.29 us (1%)
    pallas_call x1, Pallas kernels, body(): pl.pallas_call(functools.partial(kernel, row_dev * lax.axis_size('ind')),...  110 us

profile of v3, /device:TPU:8, one launch (start us, length us, event | category | flops | bytes accessed | tf_op | source)
XLA Modules:
  0.0 112.8 jit_solution(13116788297786965485)
XLA Ops:
  1.3 110.0 %elastic_net_step.1 = (f32[32,192]{1,0:T(8,128)}, f32[32,512]{1,0:T(8,128)}, f32[32,64]{1,0:T(8,128)}, f32[1,32]{1,0:T(1,128)}, f32[1,32]{1,0:T(1,128)}) custom-call(bf16[8,4,2,256,256]{4,3,2,1,0:T(8,128)(2,1)} %bitcast.6, f32[32,16384]{1,0:T(8,128)} %phenotypes.1, s32[1,256]{1,0:T(1,128)} %screen_ids.1, s32[1,1]{1,0:T(1,128)} %bitcast.5.screen_counts, ...), custom_call_target="tpu_custom_call" | custom-call | flops 1610612736 | bytes 8388608 | tf_op jit(solution)/shard_map/elastic_net_step/pallas_call | solution.py:314
  111.3 1.5 %hand_over.1 = (f32[32,192]{1,0:T(8,128)}, f32[32,512]{1,0:T(8,128)}, f32[32,64]{1,0:T(8,128)}, f32[1,32]{1,0:T(1,128)}, f32[1,32]{1,0:T(1,128)}) custom-call(f32[32,192]{1,0:T(8,128)} %get-tuple-element.15.refs_0_, f32[32,512]{1,0:T(8,128)} %get-tuple-element.16.refs_1_, f32[32,64]{1,0:T(8,128)} %get-tuple-element.17.refs_2_, ...), custom_call_target="tpu_custom_call" | custom-call | tf_op jit(solution)/shard_map/hand_over/pallas_call | solution.py:359
